TPU v7x, 256 devices: a whole 4x4x8 slice. The times are simulated.
256 devices in a mesh: dp: 16 (over y, x), ctx: 16 (over z, core).
Axes of the slice: x: 4, y: 4, z: 8, core: 2. Of those that a mesh axis runs over, the one named last changes fastest.
Arguments:
- frames: bfloat16 [8192, 6144], P('ctx'), may hold values from -6 to 6
- proj_weight: bfloat16 [3, 6144, 4096], P(None, 'ctx', 'dp'), may hold values from -0.078125 to 0.078125
- out_weight: bfloat16 [6144, 4096], P('dp', 'ctx'), may hold values from -0.09375 to 0.09375
- query_gain: float32 [4096], P('dp'), may hold values from 0.5 to 2
- key_gain: float32 [4096], P('dp'), may hold values from 0.5 to 2
- key_tiles: int32 [32, 128, 18], P('dp', 'ctx'), may hold values from 0 to 127, as said below
- key_counts: int32 [32, 128], P('dp', 'ctx'), may hold values from 1 to 18
Outputs:
- mixed: bfloat16 [8192, 6144], P('ctx', 'dp')
Inputs may be any that keep to these rules, and one draw needn't show every extreme that they name: `key_tiles`: tiles have coordinates (frame layer, height, width) on a grid of 16 x 2 x 4, tile number (layer * 2 + height) * 4 + width. For each head and query tile, the first key_counts entries are distinct tiles that differ from the query tile by at most one in each coordinate, the query tile itself among them; the other entries repeat the query tile. In every head some tile lists its whole window.
All inputs are finite; a program needn't handle non-finite values.
Results may differ from a plain program's by a relative error of at most 0.0088.
Values may be sent and summed in bfloat16 or wider, within the bound.
A program may use at most 64 MiB of HBM per device.

v0:
```python
import jax
import jax.numpy as jnp
from jax import lax
from jax.sharding import PartitionSpec as P

TILE = 64
eps = 1e-06


def padded(block, sides, width):
    for axis, dim in sides:
        count = lax.axis_size(axis)
        forward = [(i, i + 1) for i in range(count - 1)]
        backward = [(target, source) for source, target in forward]
        low = lax.ppermute(
            lax.slice_in_dim(block, block.shape[dim] - width, None, axis=dim), axis, forward
        )
        high = lax.ppermute(lax.slice_in_dim(block, 0, width, axis=dim), axis, backward)
        block = jnp.concatenate([low, block, high], axis=dim)
    return block


def normed(rows, gain):
    stat = jnp.mean(rows * rows, axis=-1, keepdims=True)
    return rows * lax.rsqrt(stat + eps) * gain


def attend(query_rows, key_rows, value_rows, tile_ids, tile_counts, first_tile):
    heads = tile_ids.shape[0]
    slots = tile_ids.shape[2]
    head_dim = query_rows.shape[1] // heads
    query_tiles = query_rows.reshape(-1, TILE, heads, head_dim).transpose(2, 0, 1, 3)
    key_tiles = key_rows.reshape(-1, TILE, heads, head_dim).transpose(2, 0, 1, 3)
    value_tiles = value_rows.reshape(-1, TILE, heads, head_dim).transpose(2, 0, 1, 3)
    local_ids = tile_ids - first_tile
    picked_keys = jax.vmap(lambda lookup, indices: lookup[indices])(key_tiles, local_ids)
    picked_values = jax.vmap(lambda lookup, indices: lookup[indices])(value_tiles, local_ids)
    count_q = query_tiles.shape[1]
    picked_keys = picked_keys.reshape(heads, count_q, slots * TILE, head_dim)
    picked_values = picked_values.reshape(heads, count_q, slots * TILE, head_dim)
    scores = jnp.einsum(
        "hqtd,hqsd->hqts", query_tiles, picked_keys, preferred_element_type=jnp.float32
    ) * head_dim ** (-0.5)
    live = (jnp.arange(slots, dtype=jnp.int32)[None, None, :] < tile_counts[:, :, None]).astype(
        jnp.float32
    )
    live = jnp.repeat(live, TILE, axis=2)[:, :, None, :]
    weights = jnp.exp(scores) * live
    totals = jnp.sum(weights, axis=-1, keepdims=True)
    summed = (
        jnp.einsum(
            "hqts,hqsd->hqtd",
            weights.astype(jnp.bfloat16),
            picked_values,
            preferred_element_type=jnp.float32,
        )
        / totals
    )
    return summed.astype(jnp.bfloat16).transpose(1, 2, 0, 3).reshape(-1, heads * head_dim)


def body(frames, proj_weight, out_weight, query_gain, key_gain, key_tiles, key_counts):
    heads = key_tiles.shape[0]
    width = proj_weight.shape[2]
    head_dim = width // heads
    layer_tiles = key_tiles.shape[1]
    tok_count = frames.shape[0]
    columns = frames
    proj = jnp.einsum(
        "tn,cnw->ctw",
        columns,
        lax.all_gather(proj_weight, "ctx", axis=1, tiled=True),
        preferred_element_type=jnp.float32,
    )
    query_rows = normed(proj[0].reshape(-1, heads, head_dim), query_gain.reshape(heads, head_dim))
    key_rows = normed(proj[1].reshape(-1, heads, head_dim), key_gain.reshape(heads, head_dim))
    query_rows = query_rows.reshape(-1, width).astype(jnp.bfloat16)
    key_rows = key_rows.reshape(-1, width).astype(jnp.bfloat16)
    value_rows = proj[2].astype(jnp.bfloat16)
    paired = jnp.stack([key_rows, value_rows], axis=0)
    widened = padded(paired, (("ctx", 1),), tok_count)
    first_tile = (lax.axis_index("ctx") - 1) * layer_tiles
    attended = attend(query_rows, widened[0], widened[1], key_tiles, key_counts, first_tile)
    out_columns = lax.all_gather(out_weight, "ctx", axis=1, tiled=True)
    columns = out_columns
    mixed = lax.dot_general(
        lax.all_gather(attended, "dp", axis=1, tiled=True),
        columns,
        (((1,), (1,)), ((), ())),
        preferred_element_type=jnp.float32,
    )
    return mixed.astype(jnp.bfloat16)


def solution(mesh):
    placed = (
        P("ctx", None),
        P(None, "ctx", "dp"),
        P("dp", "ctx"),
        P("dp"),
        P("dp"),
        P("dp", "ctx", None),
        P("dp", "ctx"),
    )
    return jax.shard_map(
        body, mesh=mesh, in_specs=placed, out_specs=P("ctx", "dp"), check_vma=False
    )
```

profile of v0, /device:TPU:1, one launch (start us, length us, event | category | flops | bytes accessed | tf_op | source)
XLA Modules:
  0.0 201.2 jit_solution(7556137137856312792)
XLA Ops:
  6.5 0.0 all-gather.4.cloned.1.call-start
  6.5 2.1 %copy.12 = bf16[3,384,256]{1,2,0:T(8,128)(2,1)} copy(bf16[3,384,256]{2,1,0:T(8,128)(2,1)} %param.8) | data formatting | bytes 1179648 | tf_op args[1]
  8.7 0.0 all-gather.4.cloned.1.call-update
  8.7 0.0 all-gather.8.cloned.1.call-start
  8.8 0.7 all-gather.8.cloned.1.call-update
  9.5 0.0 all-gather.6.cloned.1.call-start
  9.5 0.7 fusion.23
  10.2 0.0 copy-start.1
  10.2 64.0 %all-gather.4.cloned.1.call-done = bf16[3,6144,256]{1,2,0:T(8,128)(2,1)} async-done(((bf16[3,384,256]{1,2,0:T(8,128)(2,1)}), bf16[3,6144,256]{1,2,0:T(8,128)(2,1)}) %all-gather.4.cloned.1.call-update) | async-done | bytes 9437200 | tf_op jit(solution)/shard_map/all_gather | solution.py:72
  74.2 9.5 %fusion.4 = f32[3,512,256]{1,2,0:T(8,128)S(1)} fusion(bf16[3,6144,256]{1,2,0:T(8,128)(2,1)} %all-gather.4.cloned.1.call-done, bf16[512,6144]{1,0:T(8,128)(2,1)} %param.7), kind=kOutput, calls=%fused_computation.9 | convolution fusion | flops 4831838208 | bytes 17301504 | tf_op jit(solution)/shard_map/tn,cnw->ctw/dot_general | solution.py:69
  83.7 0.0 copy-start.3
  83.8 0.0 copy-start.2
  83.8 0.1 reduce_sum.28
  83.9 0.0 copy-done.1
  83.9 0.2 slice_multiply_fusion.1
  84.1 0.1 pad_maximum_fusion.1
  84.2 1.9 collective-permute-start
  86.1 3.4 %collective-permute-start.1 = (bf16[2,512,256]{1,2,0:T(8,128)(2,1)S(1)}, bf16[2,512,256]{1,2,0:T(8,128)(2,1)}, u32[]{:S(2)}, u32[]{:S(2)}) collective-permute-start(bf16[2,512,256]{1,2,0:T(8,128)(2,1)S(1)} %pad_maximum_fusion.1), channel_id=1, source_target_pairs={{1,0},{2,1},{3,2},{4,3},{5,4},{6,5},{7,6},{8,7},{9,8},{10,9},{11,1... | collective-permute-start | bytes 1572872 | tf_op jit(solution)/shard_map/ppermute | solution.py:18
  89.5 0.0 copy-done.3
  89.5 0.1 fusion.24
  89.5 0.1 reshape.68
  89.6 0.1 broadcast_in_dim.5
  89.7 0.1 mul.100
  89.8 0.2 copy.13
  90.0 0.3 reshape_squeeze.10
  90.3 0.1 reduce_sum.27
  90.4 0.1 copy.14
  90.6 0.0 copy-done.2
  90.6 0.7 fusion.18
  91.3 3.3 %collective-permute-done = bf16[2,512,256]{1,2,0:T(8,128)(2,1)} collective-permute-done((bf16[2,512,256]{1,2,0:T(8,128)(2,1)S(1)}, bf16[2,512,256]{1,2,0:T(8,128)(2,1)}, u32[]{:S(2)}, u32[]{:S(2)}) %collective-permute-start) | collective-permute-done | bytes 524320 | tf_op jit(solution)/shard_map/ppermute | solution.py:15
  94.6 4.4 %collective-permute-done.1 = bf16[2,512,256]{1,2,0:T(8,128)(2,1)} collective-permute-done((bf16[2,512,256]{1,2,0:T(8,128)(2,1)S(1)}, bf16[2,512,256]{1,2,0:T(8,128)(2,1)}, u32[]{:S(2)}, u32[]{:S(2)}) %collective-permute-start.1) | collective-permute-done | bytes 524320 | tf_op jit(solution)/shard_map/ppermute | solution.py:18
  99.0 1.3 pad_maximum_fusion
  100.3 1.0 fusion.25
  101.3 0.9 reshape.88
  102.2 1.0 copy.16
  103.2 2.4 %reshape.89 = bf16[24,64,2,128]{1,0,3,2:T(8,128)(2,1)S(1)} reshape(bf16[1,1536,256]{1,2,0:T(8,128)(2,1)} %get-tuple-element.9) | data formatting | bytes 1572864 | tf_op jit(solution)/shard_map/reshape;squeeze | solution.py:34
  105.6 1.0 copy.19
  106.6 6.4 %gather_fusion = bf16[288,64,128]{2,1,0:T(8,128)(2,1)} fusion(bf16[2,24,64,128]{3,2,1,0:T(8,128)(2,1)S(1)} %bitcast.53, s32[288]{0:T(512)S(1)} %reshape.68), kind=kCustom, calls=%fused_computation | custom fusion | bytes 9439488 | tf_op jit(solution)/shard_map/vmap()/gather | solution.py:36
  113.0 6.3 %gather_fusion.1 = bf16[288,64,128]{2,1,0:T(8,128)(2,1)} fusion(bf16[2,24,64,128]{3,2,1,0:T(8,128)(2,1)S(1)} %bitcast.54, s32[288]{0:T(512)S(1)} %reshape.68), kind=kCustom, calls=%fused_computation.1 | custom fusion | bytes 9439488 | tf_op jit(solution)/shard_map/vmap()/gather | solution.py:37
  119.3 0.0 copy-start
  119.3 4.5 %fusion.26 = (f32[2,8,64]{2,1,0:T(8,128)S(1)}, bf16[2,8,64,1152]{3,2,1,0:T(8,128)(2,1)S(1)}) fusion(f32[2,8,1152]{2,1,0:T(8,128)S(1)} %mul.100, bf16[2,8,1152,128]{3,2,1,0:T(8,128)(2,1)} %bitcast.56, bf16[2,8,64,128]{3,0,2,1:T(2,128)(2,1)S(1)} %fusion.18), kind=kOutput, calls=%fused_computation.35 | convolution fusion | flops 306707456 | bytes 7417856 | tf_op jit(solution)/shard_map/hqtd,hqsd->hqts/dot_general | solution.py:41
  123.8 0.0 copy-done
  123.8 1.1 fusion.13
  124.9 0.3 copy.20
  125.2 0.7 copy.31
  125.9 0.0 all-gather.6.cloned.1.call-update
  126.0 0.0 all-gather.8.cloned.1.call-done
  126.0 62.4 %all-gather.6.cloned.1.call-done = bf16[512,4096]{1,0:T(8,128)(2,1)} async-done(((bf16[512,256]{1,0:T(8,128)(2,1)}), bf16[512,4096]{1,0:T(8,128)(2,1)}) %all-gather.6.cloned.1.call-update) | async-done | bytes 4194320 | tf_op jit(solution)/shard_map/all_gather | solution.py:87
  188.4 6.3 %convolution_convert_fusion = bf16[512,384]{1,0:T(8,128)(2,1)} fusion(bf16[512,4096]{1,0:T(8,128)(2,1)} %all-gather.6.cloned.1.call-done, bf16[384,4096]{1,0:T(8,128)(2,1)} %all-gather.8.cloned.1.call-done), kind=kOutput, calls=%fused_computation.10 | convolution fusion | flops 1610809344 | bytes 7733248 | tf_op jit(solution)/shard_map/dot_general | solution.py:86
  (4 shorter events, 0.1 us)
Async XLA Ops:
  6.5 67.6 %all-gather.4.cloned.1.call-start = ((), (), s32[]{:S(2)}) async-start(), calls=%async_computation | async-start | bytes 10027008 | tf_op jit(solution)/shard_map/all_gather | solution.py:72
  8.7 117.3 %all-gather.8.cloned.1.call-start = ((), (), s32[]{:S(2)}) async-start(), calls=%async_computation.2 | async-start | bytes 3342336 | tf_op jit(solution)/shard_map/all_gather | solution.py:84
  9.5 178.9 %all-gather.6.cloned.1.call-start = ((), (), s32[]{:S(2)}) async-start(), calls=%async_computation.1 | async-start | bytes 4456448 | tf_op jit(solution)/shard_map/all_gather | solution.py:87
  10.2 73.7 %copy-start.1 = (f32[256]{0:T(256)S(1)}, f32[256]{0:T(256)}, u32[]{:S(2)}) copy-start(f32[256]{0:T(256)} %param.11) | copy-start | bytes 3076
  83.7 5.8 %copy-start.3 = (s32[2,8]{1,0:T(2,128)S(1)}, s32[2,8]{1,0:T(2,128)}, u32[]{:S(2)}) copy-start(s32[2,8]{1,0:T(2,128)} %param.13) | copy-start | bytes 196
  83.8 6.8 %copy-start.2 = (f32[256]{0:T(256)S(1)}, f32[256]{0:T(256)}, u32[]{:S(2)}) copy-start(f32[256]{0:T(256)} %param.10) | copy-start | bytes 3076
  84.2 10.4 %collective-permute-start = (bf16[2,512,256]{1,2,0:T(8,128)(2,1)S(1)}, bf16[2,512,256]{1,2,0:T(8,128)(2,1)}, u32[]{:S(2)}, u32[]{:S(2)}) collective-permute-start(bf16[2,512,256]{1,2,0:T(8,128)(2,1)S(1)} %pad_maximum_fusion.1), channel_id=1, source_target_pairs={{0,1},{1,2},{2,3},{3,4},{4,5},{5,6},{6,7},{7,8},{8,9},{9,10},{10,1... | collective-permute-start | bytes 1572872 | tf_op jit(solution)/shard_map/ppermute | solution.py:15
  86.1 12.9 %collective-permute-start.1 = (bf16[2,512,256]{1,2,0:T(8,128)(2,1)S(1)}, bf16[2,512,256]{1,2,0:T(8,128)(2,1)}, u32[]{:S(2)}, u32[]{:S(2)}) collective-permute-start(bf16[2,512,256]{1,2,0:T(8,128)(2,1)S(1)} %pad_maximum_fusion.1), channel_id=1, source_target_pairs={{1,0},{2,1},{3,2},{4,3},{5,4},{6,5},{7,6},{8,7},{9,8},{10,9},{11,1... | collective-permute-start | bytes 1572872 | tf_op jit(solution)/shard_map/ppermute | solution.py:18
  119.3 4.5 %copy-start = (bf16[288,64,128]{2,1,0:T(8,128)(2,1)S(1)}, bf16[288,64,128]{2,1,0:T(8,128)(2,1)}, u32[]{:S(2)}) copy-start(bf16[288,64,128]{2,1,0:T(8,128)(2,1)} %gather_fusion.1) | copy-start | bytes 14155780
Sparse Core Ops, SparseCore 0:
  9.1 64.9 all-gather.3
  75.9 45.6 all-gather.7
  126.1 62.2 all-gather.5
where the time goes:
time: 202 us; the launch traced here: 201 us
  waiting for transfers between devices  135 us (67%)
  local copies, waits for them, and re-layouts  23 us (11%)
  matrix products  21.4 us (11%)
  between operations  13.3 us (7%)
  starting transfers between devices  5.36 us (3%)
  other arithmetic  3.22 us (2%)
    all_gather x1, waiting for transfers between devices, body(): lax.all_gather(proj_weight, 'ctx', axis=1, tiled=True)  64 us
    all_gather x1, waiting for transfers between devices, body(): lax.all_gather(attended, 'dp', axis=1, tiled=True)  62.4 us
    gather x3, local copies, waits for them, and re-layouts, attend(): lookup[indices]  12.7 us
    dot_general x1, matrix products, body(): jnp.einsum('tn,cnw->ctw', columns, lax.all_gather(proj_weight, 'ctx', axi...  9.52 us
    dot_general x1, matrix products, body(): lax.dot_general(lax.all_gather(attended, 'dp', axis=1, tiled=True), colum...  6.26 us
    dot_general x1, matrix products, attend(): jnp.einsum('hqtd,hqsd->hqts', query_tiles, picked_keys, preferred_element...  4.49 us
    ppermute x1, waiting for transfers between devices, padded(): lax.ppermute(lax.slice_in_dim(block, 0, width, axis=dim), axis, backward)  4.43 us
  transfers between devices with their start and end apart: 5, of which 4 were waited for; matrix products, arithmetic and copies ran while one was open for 19% of the time, Pallas kernels for 0%

commit v1 on v0

--- a/solution.py
+++ b/solution.py
@@ -5,6 +5,14 @@
 
 TILE = 64
 eps = 1e-06
+
+
+def try_all_runs(my_tile, dim_i):
+    part_now = jnp.concatenate(
+        lax.all_to_all(jnp.stack([my_tile for _ in range(lax.axis_size("ctx"))]), "ctx", 0, 0),
+        axis=dim_i,
+    )
+    return part_now
 
 
 def padded(block, sides, width):
@@ -69,7 +77,7 @@
     proj = jnp.einsum(
         "tn,cnw->ctw",
         columns,
-        lax.all_gather(proj_weight, "ctx", axis=1, tiled=True),
+        try_all_runs(proj_weight, dim_i=1),
         preferred_element_type=jnp.float32,
     )
     query_rows = normed(proj[0].reshape(-1, heads, head_dim), query_gain.reshape(heads, head_dim))

time: 202 us -> 379 us (1.88)
  waiting for transfers between devices: 135 us -> 289 us
  local copies, waits for them, and re-layouts: 23 us -> 36.5 us
  starting transfers between devices: 5.36 us -> 15.5 us
    all_to_all x0 -> x1, waiting for transfers between devices: none -> 220 us  [try_all_runs(): lax.all_to_all(jnp.stack([my_tile for _ in range(lax.axis_size('ctx'))]),...]
    all_gather x1 -> x0, waiting for transfers between devices: 64 us -> none  [body(): lax.all_gather(proj_weight, 'ctx', axis=1, tiled=True)]
    all_to_all x0 -> x1, starting transfers between devices: none -> 10.1 us  [try_all_runs(): lax.all_to_all(jnp.stack([my_tile for _ in range(lax.axis_size('ctx'))]),...]
    reshape x0 -> x1, local copies, waits for them, and re-layouts: none -> 9.08 us  [try_all_runs(): jnp.concatenate(lax.all_to_all(jnp.stack([my_tile for _ in range(lax.axis...]
    another operation x0 -> x1, local copies, waits for them, and re-layouts: none -> 5.15 us  [try_all_runs(): jnp.stack([my_tile for _ in range(lax.axis_size('ctx'))])]
  transfers between devices with their start and end apart: 5 -> 5, of which waited for: 4 -> 4; matrix products, arithmetic and copies ran while one was open for 19% -> 13% of each run, Pallas kernels for 0% -> 0%
where the time goes in v1:
time: 379 us; the launch traced here: 378 us
  waiting for transfers between devices  289 us (76%)
  local copies, waits for them, and re-layouts  36.5 us (10%)
  matrix products  21.4 us (6%)
  starting transfers between devices  15.5 us (4%)
  between operations  13.6 us (4%)
    all_to_all x1, waiting for transfers between devices, try_all_runs(): lax.all_to_all(jnp.stack([my_tile for _ in range(lax.axis_size('ctx'))]),...  220 us
    all_gather x1, waiting for transfers between devices, body(): lax.all_gather(attended, 'dp', axis=1, tiled=True)  62.1 us
    gather x3, local copies, waits for them, and re-layouts, attend(): lookup[indices]  12.7 us
    all_to_all x1, starting transfers between devices, try_all_runs(): lax.all_to_all(jnp.stack([my_tile for _ in range(lax.axis_size('ctx'))]),...  10.1 us
    dot_general x1, matrix products, body(): jnp.einsum('tn,cnw->ctw', columns, try_all_runs(proj_weight, dim_i=1), pr...  9.53 us
    reshape x1, local copies, waits for them, and re-layouts, try_all_runs(): jnp.concatenate(lax.all_to_all(jnp.stack([my_tile for _ in range(lax.axis...  9.08 us
  transfers between devices with their start and end apart: 5, of which 4 were waited for; matrix products, arithmetic and copies ran while one was open for 13% of the time, Pallas kernels for 0%

profile of v1, /device:TPU:1, one launch (start us, length us, event | category | flops | bytes accessed | tf_op | source)
XLA Modules:
  0.0 378.1 jit_solution(3663708350910387252)
XLA Ops:
  6.5 1.4 copy.21
  7.9 5.2 %stack.4 = bf16[16,3,384,256]{2,3,1,0:T(8,128)(2,1)} broadcast(bf16[3,384,256]{1,2,0:T(8,128)(2,1)S(1)} %copy.21), dimensions={1,2,3} | broadcast | bytes 10027008 | tf_op jit(solution)/shard_map/stack | solution.py:12
  13.1 0.0 copy-start.1
  13.1 10.1 %all-to-all-start = ((bf16[16,3,384,256]{2,3,1,0:T(8,128)(2,1)}), bf16[16,3,384,256]{2,3,1,0:T(8,128)(2,1)}, u32[]{:S(2)}, u32[]{:S(2)}) async-start(bf16[16,3,384,256]{2,3,1,0:T(8,128)(2,1)} %stack.4), calls=%async_computation | async-start | bytes 18874368 | tf_op jit(solution)/shard_map/all_to_all | solution.py:12
  23.2 0.0 all-gather.5.cloned.1.call-start
  23.2 0.7 all-gather.5.cloned.1.call-update
  23.9 0.0 all-gather.3.cloned.1.call-start
  24.0 0.0 copy-done.1
  24.0 219.9 %all-to-all-done = bf16[16,3,384,256]{2,3,1,0:T(8,128)(2,1)} async-done(((bf16[16,3,384,256]{2,3,1,0:T(8,128)(2,1)}), bf16[16,3,384,256]{2,3,1,0:T(8,128)(2,1)}, u32[]{:S(2)}, u32[]{:S(2)}) %all-to-all-start) | async-done | bytes 9437216 | tf_op jit(solution)/shard_map/all_to_all | solution.py:12
  243.8 9.1 %copy.35 = bf16[16,3,32,8,384]{4,3,0,2,1:T(8,128)(2,1)} copy(bf16[16,3,32,8,384]{4,3,2,1,0:T(8,128)(2,1)} %bitcast.16) | data formatting | bytes 18874368 | tf_op jit(solution)/shard_map/reshape | solution.py:11
  252.9 0.0 copy-start.2
  252.9 9.5 %fusion.4 = f32[3,512,256]{1,2,0:T(8,128)S(1)} fusion(bf16[3,6144,256]{1,2,0:T(8,128)(2,1)} %bitcast.58, bf16[512,6144]{1,0:T(8,128)(2,1)} %param.7), kind=kOutput, calls=%fused_computation.9 | convolution fusion | flops 4831838208 | bytes 17301504 | tf_op jit(solution)/shard_map/tn,cnw->ctw/dot_general | solution.py:77
  262.5 0.0 copy-start.4
  262.5 0.0 copy-start.3
  262.6 0.1 reduce_sum.28
  262.6 0.0 copy-done.2
  262.6 0.2 slice_multiply_fusion.1
  262.9 0.1 pad_maximum_fusion.1
  262.9 2.4 collective-permute-start
  265.3 2.9 collective-permute-start.1
  268.2 0.0 copy-done.4
  268.2 0.1 fusion.24
  268.3 0.1 reshape.78
  268.4 0.1 broadcast_in_dim.5
  268.5 0.1 mul.100
  268.6 0.2 copy.23
  268.8 0.3 reshape_squeeze.10
  269.1 0.1 reduce_sum.27
  269.1 0.1 copy.24
  269.3 0.0 copy-done.3
  269.3 0.7 fusion.18
  270.0 1.4 collective-permute-done
  271.4 4.5 %collective-permute-done.1 = bf16[2,512,256]{1,2,0:T(8,128)(2,1)} collective-permute-done((bf16[2,512,256]{1,2,0:T(8,128)(2,1)S(1)}, bf16[2,512,256]{1,2,0:T(8,128)(2,1)}, u32[]{:S(2)}, u32[]{:S(2)}) %collective-permute-start.1) | collective-permute-done | bytes 524320 | tf_op jit(solution)/shard_map/ppermute | solution.py:26
  275.9 1.3 pad_maximum_fusion
  277.3 1.0 fusion.25
  278.2 0.9 reshape.98
  279.2 1.0 copy.26
  280.2 2.4 reshape.99
  282.6 1.0 copy.29
  283.5 6.4 %gather_fusion = bf16[288,64,128]{2,1,0:T(8,128)(2,1)} fusion(bf16[2,24,64,128]{3,2,1,0:T(8,128)(2,1)S(1)} %bitcast.56, s32[288]{0:T(512)S(1)} %reshape.78), kind=kCustom, calls=%fused_computation | custom fusion | bytes 9439488 | tf_op jit(solution)/shard_map/vmap()/gather | solution.py:44
  289.9 6.3 %gather_fusion.1 = bf16[288,64,128]{2,1,0:T(8,128)(2,1)} fusion(bf16[2,24,64,128]{3,2,1,0:T(8,128)(2,1)S(1)} %bitcast.57, s32[288]{0:T(512)S(1)} %reshape.78), kind=kCustom, calls=%fused_computation.1 | custom fusion | bytes 9439488 | tf_op jit(solution)/shard_map/vmap()/gather | solution.py:45
  296.2 0.0 copy-start
  296.2 4.5 %fusion.26 = (f32[2,8,64]{2,1,0:T(8,128)S(1)}, bf16[2,8,64,1152]{3,2,1,0:T(8,128)(2,1)S(1)}) fusion(f32[2,8,1152]{2,1,0:T(8,128)S(1)} %mul.100, bf16[2,8,1152,128]{3,2,1,0:T(8,128)(2,1)} %bitcast.60, bf16[2,8,64,128]{3,0,2,1:T(2,128)(2,1)S(1)} %fusion.18), kind=kOutput, calls=%fused_computation.35 | convolution fusion | flops 306707456 | bytes 7417856 | tf_op jit(solution)/shard_map/hqtd,hqsd->hqts/dot_general | solution.py:49
  300.7 0.0 copy-done
  300.7 1.1 fusion.13
  301.8 0.3 copy.30
  302.1 0.7 copy.42
  302.8 0.0 all-gather.3.cloned.1.call-update
  302.9 0.0 all-gather.5.cloned.1.call-done
  302.9 62.1 %all-gather.3.cloned.1.call-done = bf16[512,4096]{1,0:T(8,128)(2,1)} async-done(((bf16[512,256]{1,0:T(8,128)(2,1)}), bf16[512,4096]{1,0:T(8,128)(2,1)}) %all-gather.3.cloned.1.call-update) | async-done | bytes 4194320 | tf_op jit(solution)/shard_map/all_gather | solution.py:95
  365.0 6.3 %convolution_convert_fusion = bf16[512,384]{1,0:T(8,128)(2,1)} fusion(bf16[512,4096]{1,0:T(8,128)(2,1)} %all-gather.3.cloned.1.call-done, bf16[384,4096]{1,0:T(8,128)(2,1)} %all-gather.5.cloned.1.call-done), kind=kOutput, calls=%fused_computation.10 | convolution fusion | flops 1610809344 | bytes 7733248 | tf_op jit(solution)/shard_map/dot_general | solution.py:94
  (5 shorter events, 0.1 us)
Async XLA Ops:
  13.1 10.9 %copy-start.1 = (s32[2,8,18]{2,1,0:T(8,128)S(1)}, s32[2,8,18]{2,1,0:T(8,128)}, u32[]{:S(2)}) copy-start(s32[2,8,18]{2,1,0:T(8,128)} %param.12) | copy-start | bytes 3460
  13.1 230.8 %all-to-all-start = ((bf16[16,3,384,256]{2,3,1,0:T(8,128)(2,1)}), bf16[16,3,384,256]{2,3,1,0:T(8,128)(2,1)}, u32[]{:S(2)}, u32[]{:S(2)}) async-start(bf16[16,3,384,256]{2,3,1,0:T(8,128)(2,1)} %stack.4), calls=%async_computation | async-start | bytes 18874368 | tf_op jit(solution)/shard_map/all_to_all | solution.py:12
  23.2 279.7 %all-gather.5.cloned.1.call-start = ((), (), s32[]{:S(2)}) async-start(), calls=%async_computation.2 | async-start | bytes 3342336 | tf_op jit(solution)/shard_map/all_gather | solution.py:92
  23.9 341.1 %all-gather.3.cloned.1.call-start = ((), (), s32[]{:S(2)}) async-start(), calls=%async_computation.1 | async-start | bytes 4456448 | tf_op jit(solution)/shard_map/all_gather | solution.py:95
  252.9 9.7 %copy-start.2 = (f32[256]{0:T(256)S(1)}, f32[256]{0:T(256)}, u32[]{:S(2)}) copy-start(f32[256]{0:T(256)} %param.11) | copy-start | bytes 3076
  262.5 5.8 %copy-start.4 = (s32[2,8]{1,0:T(2,128)S(1)}, s32[2,8]{1,0:T(2,128)}, u32[]{:S(2)}) copy-start(s32[2,8]{1,0:T(2,128)} %param.13) | copy-start | bytes 196
  262.5 6.8 %copy-start.3 = (f32[256]{0:T(256)S(1)}, f32[256]{0:T(256)}, u32[]{:S(2)}) copy-start(f32[256]{0:T(256)} %param.10) | copy-start | bytes 3076
  262.9 8.5 %collective-permute-start = (bf16[2,512,256]{1,2,0:T(8,128)(2,1)S(1)}, bf16[2,512,256]{1,2,0:T(8,128)(2,1)}, u32[]{:S(2)}, u32[]{:S(2)}) collective-permute-start(bf16[2,512,256]{1,2,0:T(8,128)(2,1)S(1)} %pad_maximum_fusion.1), channel_id=1, source_target_pairs={{0,1},{1,2},{2,3},{3,4},{4,5},{5,6},{6,7},{7,8},{8,9},{9,10},{10,1... | collective-permute-start | bytes 1572872 | tf_op jit(solution)/shard_map/ppermute | solution.py:23
  265.3 10.6 %collective-permute-start.1 = (bf16[2,512,256]{1,2,0:T(8,128)(2,1)S(1)}, bf16[2,512,256]{1,2,0:T(8,128)(2,1)}, u32[]{:S(2)}, u32[]{:S(2)}) collective-permute-start(bf16[2,512,256]{1,2,0:T(8,128)(2,1)S(1)} %pad_maximum_fusion.1), channel_id=1, source_target_pairs={{1,0},{2,1},{3,2},{4,3},{5,4},{6,5},{7,6},{8,7},{9,8},{10,9},{11,1... | collective-permute-start | bytes 1572872 | tf_op jit(solution)/shard_map/ppermute | solution.py:26
  296.2 4.5 %copy-start = (bf16[288,64,128]{2,1,0:T(8,128)(2,1)S(1)}, bf16[288,64,128]{2,1,0:T(8,128)(2,1)}, u32[]{:S(2)}) copy-start(bf16[288,64,128]{2,1,0:T(8,128)(2,1)} %gather_fusion.1) | copy-start | bytes 14155780
Sparse Core Ops, SparseCore 0:
  25.8 112.1 all-gather.4
  303.0 61.9 all-gather.2
